TPU v7x, 32 devices: a whole 2x2x4 slice. The times are simulated.
32 devices in a mesh: groups: 2 (over y), layer: 4 (over z), latent: 4 (over x, core).
Axes of the slice: x: 2, y: 2, z: 4, core: 2. Of those that a mesh axis runs over, the one named last changes fastest.
Arguments:
- residuals: bfloat16 [4, 256, 2304], P('layer', 'groups'), parts along dimension 1, may hold values from -6 to 6
- targets: bfloat16 [4, 256, 2304], P('layer', 'groups'), parts along dimension 1, may hold values from -6 to 6
- enc_weight: bfloat16 [4, 2304, 8192], P('layer', None, 'latent'), may hold values from -0.125 to 0.125
- enc_bias: float32 [4, 8192], P('layer', 'latent'), may hold values from -2.5 to 2.5
- dec_weight: bfloat16 [4, 8192, 2304], P('layer', 'latent'), may hold values from -0.0625 to 0.0625
- out_gain: float32 [4, 2304], P('layer'), may hold values from 0.1 to 1.9
- block_list: int32 [4, 2, 24], P('layer', 'groups'), parts along dimension 1, may hold values from 0 to 63, as said below
- block_count: int32 [4, 2], P('layer', 'groups'), parts along dimension 1, may hold values from 1 to 24
Outputs:
- recon: bfloat16 [4, 256, 2304], P('layer', 'groups', 'latent'), parts along dimension 1
- code_grad: bfloat16 [4, 256, 8192], P('layer', 'groups', 'latent'), parts along dimension 1
- layer_loss: float32 [2, 4], P('groups', 'layer'), parts along dimension 0
There are 2 independent parts, one for each index of `groups`. A program takes and returns all parts, laid end to end along the dimension named above; an argument that names none is the same for every part. Nothing has to cross between parts.
Inputs may be any that keep to these rules, and one draw needn't show every extreme that they name: `block_list`: within the first block_count entries of a row the blocks are distinct; later entries are unused.
All inputs are finite; a program needn't handle non-finite values.
Results may differ from a plain program's by a relative error of at most 0.0054.
Values may be sent and summed in bfloat16 or wider, within the bound.
No kernel may reach another device: no remote copies, remote signals or barrier semaphores. Data moves between devices by JAX's collectives and lax.ppermute only.
A program may use at most 128 MiB of HBM per device.

v0:
```python
import functools

import jax
import jax.numpy as jnp
from jax import lax
from jax.experimental import pallas as pl
from jax.experimental.pallas import tpu as pltpu
from jax.sharding import PartitionSpec as P

BLOCK = 128
PAIR = 2 * BLOCK
KEPT = 2
F32 = jnp.float32
BF16 = jnp.bfloat16


def encode_decode(
    list_any, count_ref, x_any, bias_any, target_any, gain_any, enc_ref, dec_ref,
    keep_ref, send_ref, ids_ref, beside_ref, own_gain_ref,
    list_ref, x_ref, bias_ref, target_ref, gain_ref, enc_held, dec_held, codes, total, in_sem, enc_sem, dec_sem,
):
    blocks = enc_ref.shape[1] // BLOCK
    list_load = pltpu.make_async_copy(list_any, list_ref, in_sem.at[0])
    list_load.start()
    where = lax.axis_index("latent")
    first = where * blocks
    core = lax.rem(where, 2)
    rows = keep_ref.shape[0]
    mine = pl.ds(pl.multiple_of(core * rows, rows), rows)
    loads = [
        pltpu.make_async_copy(x_any, x_ref, in_sem.at[1]),
        pltpu.make_async_copy(bias_any, bias_ref, in_sem.at[2]),
        pltpu.make_async_copy(target_any.at[mine, :], target_ref, in_sem.at[3]),
        pltpu.make_async_copy(gain_any, gain_ref, in_sem.at[4]),
    ]
    for load in loads:
        load.start()
    total[...] = jnp.zeros_like(total)

    def place_of(n):
        return lax.div(n, 4), pl.ds(pl.multiple_of(lax.rem(n, 4) * BLOCK, BLOCK), BLOCK)

    def rows_of(n):
        return pl.ds(pl.multiple_of(ids_ref[0, n] * BLOCK, BLOCK), BLOCK)

    def enc_copy(n):
        quad, place = place_of(n)
        return pltpu.make_async_copy(enc_ref.at[:, rows_of(n)], enc_held.at[quad, :, place], enc_sem.at[n])

    def dec_copy(n):
        quad, place = place_of(n)
        return pltpu.make_async_copy(dec_ref.at[rows_of(n), :], dec_held.at[quad, place, :], dec_sem.at[n])

    list_load.wait()
    count = count_ref[0, 0]

    def look(slot, n):
        block = list_ref[0, 0, slot] - first
        live = (slot < count) & (block >= 0) & (block < blocks)

        @pl.when(live)
        def _():
            ids_ref[0, n] = block
            enc_copy(n).start()

        return n + live.astype(jnp.int32)

    live_count = lax.fori_loop(0, jnp.minimum(count, list_ref.shape[2]), look, jnp.int32(0))
    ids_ref[0, blocks] = live_count
    lax.fori_loop(0, live_count, lambda n, c: (dec_copy(n).start(), c)[1], 0)
    quads = lax.div(live_count + 1, 4)
    last_pair = (lax.rem(live_count, 4) == 1) | (lax.rem(live_count, 4) == 2)

    def clear(n, carry):
        quad, place = place_of(n)
        dec_held[quad, place, :] = jnp.zeros((BLOCK, dec_held.shape[2]), BF16)
        ids_ref[0, n] = ids_ref[0, 0]
        return carry

    lax.fori_loop(live_count, jnp.where(last_pair, 4 * quads + 2, 4 * quads), clear, 0)
    for load in loads:
        load.wait()

    width = own_gain_ref.shape[1]
    for chip in range(target_ref.shape[1] // width):

        @pl.when(lax.div(where, 2) == chip)
        def _(columns=slice(chip * width, (chip + 1) * width)):
            beside_ref[:rows, :] = target_ref[:, columns]
            own_gain_ref[...] = gain_ref[:, columns]

    left, terms = own_gain_ref[...], []
    for _ in range(3):
        terms.append(left.astype(BF16).astype(F32))
        left = left - terms[-1]
    row = lax.broadcasted_iota(jnp.int32, (beside_ref.shape[0] - rows, width), 0)
    beside_ref[rows:, :] = sum(jnp.where(row == i, term, 0.0) for i, term in enumerate(terms)).astype(BF16)

    def encode(n, size):
        for i in range(size):
            pl.when(n + i < live_count)(lambda i=i: enc_copy(n + i).wait())
        quad = lax.div(n, 4)
        lanes = pl.ds(pl.multiple_of(lax.rem(n, 4) * BLOCK, size * BLOCK), size * BLOCK)
        bias = jnp.concatenate([bias_ref[:, rows_of(n + i)] for i in range(size)], axis=1)
        pre_act = jnp.dot(x_ref[...], enc_held[quad, :, lanes], preferred_element_type=F32) + bias
        lane = lax.broadcasted_iota(jnp.int32, pre_act.shape, 1)
        used = lane < (live_count - n) * BLOCK
        codes[quad, :, lanes] = jnp.where(used, jnp.maximum(pre_act, 0.0), 0.0).astype(BF16)

    def decode(pair, carry):
        quad, lanes = lax.div(pair, 2), pl.ds(pl.multiple_of(lax.rem(pair, 2) * PAIR, PAIR), PAIR)
        for n in (2 * pair, 2 * pair + 1):
            pl.when(n < live_count)(lambda n=n: dec_copy(n).wait())
        total[...] += jnp.dot(codes[quad, :, lanes], dec_held[quad, lanes, :], preferred_element_type=F32)
        return carry

    pairs = lax.div(live_count + 1, 2)
    fours = jnp.where(live_count <= 4, 0, quads)
    lax.fori_loop(0, fours, lambda quad, c: (encode(4 * quad, 4), c)[1], 0)
    lax.fori_loop(2 * fours, pairs, lambda pair, c: (encode(2 * pair, 2), c)[1], 0)
    lax.fori_loop(0, pairs, decode, 0)

    keep_ref[...] = total[mine, :]
    send_ref[...] = total[pl.ds(pl.multiple_of((1 - core) * rows, rows), rows), :].astype(BF16)


def finish(
    got_ref, before_ref, after_ref, all_ref, there_square_ref, after_square_ref, gain_ref, target_ref,
    message_ref, stay_ref, send_ref,
):
    got = got_ref[...].astype(F32)
    width = got.shape[1]
    low = (lax.axis_index("layer") & (lax.axis_size("layer") // 2)) == 0
    fitted = gain_ref[...] * jnp.where(low, before_ref[...], before_ref[...] + got)
    error_term = fitted - target_ref[: got.shape[0], :].astype(F32)
    squares = error_term * error_term
    added = functools.reduce(add_terms, [squares[:, i : i + BLOCK] for i in range(0, width - BLOCK + 1, BLOCK)])
    rest = width % BLOCK
    if rest:
        zeros = jnp.zeros((squares.shape[0], BLOCK - rest), F32)
        added = added + jnp.concatenate([squares[:, width - rest :], zeros], axis=1)
    entering = jnp.where(low, there_square_ref[...] * all_ref[...] + got, after_square_ref[...] * got)
    message_ref[:, :width] = (after_ref[...] + entering).astype(BF16)
    message_ref[:, width:] = added.astype(BF16)
    left, right = fitted[:, : width // 2].astype(BF16), fitted[:, width // 2 :].astype(BF16)
    first = (lax.axis_index("latent") & 1) == 0
    stay_ref[...] = jnp.where(first, left, right)
    send_ref[...] = jnp.where(first, right, left)


def add_terms(one, two):
    return one + two


def rows_of(dec_ref, block, half):
    cut = dec_ref.shape[1] // 2
    return dec_ref.at[pl.ds(pl.multiple_of(block * BLOCK, BLOCK), BLOCK), pl.ds(pl.multiple_of(half * cut, cut), cut)]


def in_quads(n):
    return lax.div(n, 4), pl.ds(pl.multiple_of(lax.rem(n, 4) * BLOCK, BLOCK), BLOCK)


def quads_of(live_count):
    rest = lax.rem(live_count, 4)
    return lax.div(live_count + 1, 4), (rest == 1) | (rest == 2)


def by_core(core, mine, theirs, held):
    rows = mine.shape[0]
    held[pl.ds(pl.multiple_of(core * rows, rows), rows), :] = mine
    held[pl.ds(pl.multiple_of((1 - core) * rows, rows), rows), :] = theirs


def times_rows(grad, rows):
    return lax.dot_general(grad, rows, (((1,), (1,)), ((), ())), preferred_element_type=F32)


def near_gradient(top, ids_ref, own_ref, near_ref, dec_ref, part_ref, far_kept, grad, dec_near, near_sem, far_sem):
    blocks = near_sem.shape[0]
    kept, _, cut = far_kept.shape
    latent = lax.axis_index("latent")
    here = lax.div(latent & top, top)
    live_count = ids_ref[0, blocks]
    far_count = jnp.minimum(live_count, 4 * kept)

    def near_copy(n):
        quad, place = in_quads(n)
        return pltpu.make_async_copy(rows_of(dec_ref, ids_ref[0, n], here), dec_near.at[quad, place, :], near_sem.at[n])

    def far_copy(n):
        quad, place = in_quads(n)
        return pltpu.make_async_copy(rows_of(dec_ref, ids_ref[0, n], 1 - here), far_kept.at[quad, place, :], far_sem.at[n])

    lax.fori_loop(0, live_count, lambda n, c: (near_copy(n).start(), c)[1], 0)
    lax.fori_loop(0, far_count, lambda n, c: (far_copy(n).start(), c)[1], 0)
    by_core(latent & 1, own_ref[:, :cut], near_ref[:, :cut], grad)

    def multiply(quad, size):
        for n in [4 * quad + i for i in range(size)]:
            pl.when(n < live_count)(lambda n=n: near_copy(n).wait())
        places = pl.ds(0, size * BLOCK)
        part_ref[quad, :, places] = times_rows(grad[...], dec_near[quad, places, :])

    quads, last_pair = quads_of(live_count)
    lax.fori_loop(0, quads, lambda quad, c: (multiply(quad, 4), c)[1], 0)
    pl.when(last_pair)(lambda: multiply(quads, 2))
    lax.fori_loop(0, far_count, lambda n, c: (far_copy(n).wait(), c)[1], 0)


def code_gradient(
    top, ids_ref, own_ref, got_ref, far_ref, stay_ref, other_ref, part_ref, far_kept, dec_ref,
    out_ref, recon_ref, mean_ref, grad, fitted, dec_far, far_sem,
):
    blocks = far_sem.shape[0]
    kept, _, cut = far_kept.shape
    latent = lax.axis_index("latent")
    there = 1 - lax.div(latent & top, top)
    core = latent & 1
    live_count = ids_ref[0, blocks]

    def far_copy(n):
        quad, place = in_quads(n)
        return pltpu.make_async_copy(rows_of(dec_ref, ids_ref[0, n], there), dec_far.at[quad - kept, place, :], far_sem.at[n])

    lax.fori_loop(4 * kept, live_count, lambda n, c: (far_copy(n).start(), c)[1], 0)
    by_core(core, got_ref[:, :cut], far_ref[:, :cut], grad)
    out_ref[...] = jnp.zeros_like(out_ref)

    def multiply(quad, size, held, offset):
        blocks_here = [4 * quad + i for i in range(size)]
        if offset:
            for n in blocks_here:
                pl.when(n < live_count)(lambda n=n: far_copy(n).wait())
        places = pl.ds(0, size * BLOCK)
        product = (part_ref[quad, :, places] + times_rows(grad[...], held[quad - offset, places, :])).astype(BF16)
        for i, n in enumerate(blocks_here):

            @pl.when(n < live_count)
            def _(i=i, n=n):
                lanes = pl.ds(pl.multiple_of(ids_ref[0, n] * BLOCK, BLOCK), BLOCK)
                out_ref[:, lanes] = product[:, i * BLOCK : (i + 1) * BLOCK]

    quads, last_pair = quads_of(live_count)
    lax.fori_loop(0, jnp.minimum(quads, kept), lambda quad, c: (multiply(quad, 4, far_kept, 0), c)[1], 0)
    lax.fori_loop(kept, quads, lambda quad, c: (multiply(quad, 4, dec_far, kept), c)[1], 0)
    pl.when(last_pair & (quads < kept))(lambda: multiply(quads, 2, far_kept, 0))
    pl.when(last_pair & (quads >= kept))(lambda: multiply(quads, 2, dec_far, kept))
    columns = stay_ref.shape[1]
    by_core(core, stay_ref[...].astype(F32), other_ref[:, :columns].astype(F32), fitted)
    recon_ref[...] = jnp.transpose(fitted[...]).astype(BF16)
    squares = sum(ref[:, cut:].astype(F32) for ref in (own_ref, got_ref, far_ref)) + other_ref[:, columns:].astype(F32)
    total = jnp.sum(jnp.sum(squares, axis=0, keepdims=True), axis=1, keepdims=True)
    mean_ref[...] = total / (grad.shape[0] * 2 * cut)


def swap(value, axis, bit):
    size = lax.axis_size(axis)
    return lax.ppermute(value, axis, [(i, i ^ bit) for i in range(size)])


def in_hbm(value):
    return pltpu.with_memory_space_constraint(value, pltpu.HBM)


def part(value, start, size, axis):
    return lax.dynamic_slice_in_dim(value, start, size, axis)


def encode_call(block_list, block_count, x, bias, targets, gain, enc, dec, width):
    tok_rows, model_width = x.shape
    local_latents = enc.shape[1]
    blocks = local_latents // BLOCK
    quad_slots = (blocks + 3) // 4
    rows = tok_rows // 2
    vmem = pl.BlockSpec(memory_space=pltpu.VMEM)
    smem = pl.BlockSpec(memory_space=pltpu.SMEM)
    anyw = pl.BlockSpec(memory_space=pl.ANY)
    return pl.pallas_call(
        encode_decode,
        out_shape=(
            pltpu.VMEM((rows, model_width), F32),
            pltpu.VMEM((rows, model_width), BF16),
            pltpu.SMEM((1, blocks + 1), jnp.int32),
            pltpu.VMEM((rows + 16, width), BF16),
            pltpu.VMEM((1, width), F32),
        ),
        in_specs=[anyw, smem] + [anyw] * 6,
        out_specs=(vmem, vmem, smem, vmem, vmem),
        scratch_shapes=[
            pltpu.SMEM(block_list.shape, jnp.int32),
            pltpu.VMEM((tok_rows, model_width), BF16),
            pltpu.VMEM((1, local_latents), F32),
            pltpu.VMEM((rows, model_width), BF16),
            pltpu.VMEM((1, model_width), F32),
            pltpu.VMEM((quad_slots, model_width, 4 * BLOCK), BF16),
            pltpu.VMEM((quad_slots, 4 * BLOCK, model_width), BF16),
            pltpu.VMEM((quad_slots, tok_rows, 4 * BLOCK), BF16),
            pltpu.VMEM((tok_rows, model_width), F32),
            pltpu.SemaphoreType.DMA((5,)),
            pltpu.SemaphoreType.DMA((blocks,)),
            pltpu.SemaphoreType.DMA((blocks,)),
        ],
        compiler_params=pltpu.CompilerParams(vmem_limit_bytes=32 << 20),
        name="encode_decode",
    )(block_list, block_count, x, bias, targets, gain, enc, dec)


def local(residuals, targets, enc_weight, enc_bias, dec_weight, out_gain, block_list, block_count):
    tok_rows, model_width = residuals.shape[1:]
    local_latents = enc_weight.shape[2]
    blocks = local_latents // BLOCK
    slots = (blocks + 3) // 4
    kept = min(KEPT, slots)
    more = max(slots - kept, 1)
    quad = 4 * BLOCK
    layers, latents = lax.axis_size("layer"), lax.axis_size("latent")
    layer, latent = lax.axis_index("layer"), lax.axis_index("latent")
    core = latent % 2
    rows = tok_rows // 2
    chips = latents // 2
    width = model_width // chips
    column = (latent // 2) * width

    layer_bits = [1 << s for s in range((layers - 1).bit_length())]
    chip_bits = [1 << s for s in range((chips - 1).bit_length(), 0, -1)]

    dec_hbm = in_hbm(dec_weight[0])
    vmem = pl.BlockSpec(memory_space=pltpu.VMEM)
    smem = pl.BlockSpec(memory_space=pltpu.SMEM)
    anyw = pl.BlockSpec(memory_space=pl.ANY)
    keep, send, ids, beside, gain = encode_call(
        in_hbm(block_list), block_count, in_hbm(residuals[0]), in_hbm(enc_bias), in_hbm(targets[0]), in_hbm(out_gain),
        in_hbm(enc_weight[0]), dec_hbm, width,
    )

    held = keep + swap(send, "latent", 1).astype(F32)
    for bit in chip_bits:
        half = held.shape[1] // 2
        upper = (latent & bit) != 0
        away = jnp.where(upper, held[:, :half], held[:, half:]).astype(BF16)
        mine = jnp.where(upper, held[:, half:], held[:, :half])
        if bit == chip_bits[-1]:
            near_beside = swap(beside, "layer", 1)
        held = mine + swap(away, "latent", bit).astype(F32)
    own = held
    near = swap(own.astype(BF16), "layer", 1).astype(F32)
    target = beside[:rows]
    near_target = near_beside[:rows]
    near_gain = sum(near_beside[rows + i : rows + i + 1].astype(F32) for i in range(3))
    square = gain * gain
    near_square = near_gain * near_gain
    all_square = square + near_square

    low = (layer & 1) == 0

    def pair_sums(own, near):
        own_error = square * own - gain * target.astype(F32)
        near_error = near_square * near - near_gain * near_target.astype(F32)
        before = jnp.where(low, own, own + near)
        after = jnp.where(low, own_error + near_square * own + near_error, own_error + square * near)
        all_after = own_error + near_error + jnp.where(low, near_square * own, square * near)
        return before, after, own + near, all_after

    before, after, all_before, all_after = pair_sums(own, near)
    after_square = jnp.where(low, square + near_square, square)
    for step in layer_bits[1:]:
        upper = (layer & step) != 0
        there_square = swap(all_square, "layer", step)
        if step == layer_bits[-1]:
            outgoing = jnp.where((layer & step) == 0, all_before, all_after).astype(BF16)
            if len(layer_bits) == 2:
                own, near, outgoing = lax.optimization_barrier((own, near, outgoing))
                before, after, all_before, _ = pair_sums(own, near)
            got = swap(outgoing, "layer", step)
            break
        there_before = swap(all_before.astype(BF16), "layer", step).astype(F32)
        there_after = swap(all_after.astype(BF16), "layer", step).astype(F32)
        before, after = (
            jnp.where(upper, before + there_before, before),
            jnp.where(upper, after + after_square * there_before, after + there_square * all_before + there_after),
        )
        after_square = jnp.where(upper, after_square, after_square + there_square)
        all_before, all_after = (
            all_before + there_before,
            all_after + there_after + jnp.where(upper, all_square * there_before, there_square * all_before),
        )
        all_square = all_square + there_square

    columns = width // 2
    message, stay, send = pl.pallas_call(
        finish,
        out_shape=(
            pltpu.VMEM((rows, width + BLOCK), BF16),
            pltpu.VMEM((rows, columns), BF16),
            pltpu.VMEM((rows, columns), BF16),
        ),
        in_specs=[vmem] * 8,
        out_specs=(vmem, vmem, vmem),
        compiler_params=pltpu.CompilerParams(vmem_limit_bytes=16 << 20),
        name="finish",
    )(got, before, after, all_before, there_square, after_square, gain, beside)

    for bit in reversed(chip_bits[1:]):
        upper = (latent & bit) != 0
        got = swap(message, "latent", bit)
        cut = message.shape[1] - BLOCK
        here, there = message[:, :cut], got[:, :cut]
        squares = (message[:, cut:].astype(F32) + got[:, cut:].astype(F32)).astype(BF16)
        message = jnp.concatenate([jnp.where(upper, there, here), jnp.where(upper, here, there), squares], axis=1)
    top, cut = chip_bits[0], model_width // 2
    got = swap(message, "latent", top)
    near = swap(message[:, :cut], "latent", 1)
    send = jnp.concatenate([send, message[:, cut:]], axis=1)
    near_part, far_kept = pl.pallas_call(
        functools.partial(near_gradient, top),
        out_shape=(pltpu.VMEM((slots, tok_rows, quad), F32), pltpu.VMEM((kept, quad, cut), BF16)),
        in_specs=[smem, vmem, vmem, anyw],
        out_specs=(vmem, vmem),
        scratch_shapes=[
            pltpu.VMEM((tok_rows, cut), BF16),
            pltpu.VMEM((slots, quad, cut), BF16),
            pltpu.SemaphoreType.DMA((blocks,)),
            pltpu.SemaphoreType.DMA((blocks,)),
        ],
        compiler_params=pltpu.CompilerParams(vmem_limit_bytes=24 << 20),
        name="near_gradient",
    )(ids, message, near, dec_hbm)
    got, near_part, send = lax.optimization_barrier((got, near_part, send))
    far = swap(got, "latent", 1)
    other = swap(send, "latent", 1)

    code_grad, recon, loss = pl.pallas_call(
        functools.partial(code_gradient, top),
        out_shape=(
            jax.ShapeDtypeStruct((tok_rows, local_latents), BF16),
            jax.ShapeDtypeStruct((columns, tok_rows), BF16),
            jax.ShapeDtypeStruct((1, 1), F32),
        ),
        in_specs=[smem] + [vmem] * 7 + [anyw],
        out_specs=(vmem, vmem, vmem),
        scratch_shapes=[
            pltpu.VMEM((tok_rows, cut), BF16),
            pltpu.VMEM((tok_rows, columns), F32),
            pltpu.VMEM((more, quad, cut), BF16),
            pltpu.SemaphoreType.DMA((blocks,)),
        ],
        compiler_params=pltpu.CompilerParams(vmem_limit_bytes=16 << 20),
        name="code_gradient",
    )(ids, message, got, far, stay, other, *[pltpu.with_memory_space_constraint(a, pltpu.VMEM) for a in (near_part, far_kept)], dec_hbm)
    return recon.T[None], code_grad[None], loss


def solution(mesh):
    placed = (
        P("layer", "groups", None),
        P("layer", "groups", None),
        P("layer", None, "latent"),
        P("layer", "latent"),
        P("layer", "latent", None),
        P("layer", None),
        P("layer", "groups", None),
        P("layer", "groups"),
    )
    return jax.shard_map(
        local,
        mesh=mesh,
        in_specs=placed,
        out_specs=(
            P("layer", "groups", "latent"),
            P("layer", "groups", "latent"),
            P("groups", "layer"),
        ),
        check_vma=False,
    )
```

profile of v0, /device:TPU:0, one launch (start us, length us, event | category | flops | bytes accessed | tf_op | source)
XLA Modules:
  0.0 38.5 jit_solution(5749169053065903062)
XLA Ops:
  1.3 3.3 %encode_decode.1 = (f32[64,2304]{1,0:T(8,128)S(1)}, bf16[64,2304]{1,0:T(8,128)(2,1)S(1)}, s32[1,17]{1,0:T(1,128)S(4)}, bf16[80,1152]{1,0:T(8,128)(2,1)S(1)}, f32[1,1152]{1,0:T(1,128)S(1)}) custom-call(s32[1,1,24]{2,1,0:T(1,128)} %list_any.1, s32[1,1]{1,0:T(1,128)S(6)} %copy.11.count_ref, bf16[128,2304]{1,0:T(8,128)(2,1)} %bitcast.12, f32[1,2048]{1,0:T(1,128)} %bias_any.1, ...), custom_call_target="tpu_custom_call" | custom-call | tf_op jit(solution)/shard_map/encode_decode/pallas_call | solution.py:279
  4.6 2.7 %collective-permute-start = (bf16[64,2304]{1,0:T(8,128)(2,1)S(1)}, bf16[64,2304]{1,0:T(8,128)(2,1)S(1)}, u32[]{:S(2)}, u32[]{:S(2)}) collective-permute-start(bf16[64,2304]{1,0:T(8,128)(2,1)S(1)} %get-tuple-element.24), channel_id=1, source_target_pairs={{0,1},{1,0},{2,3},{3,2},{4,5},{5,4},{6,7},{7,6},{8,9},{9,8},{10,11... | collective-permute-start | bytes 884744 | tf_op jit(solution)/shard_map/ppermute | solution.py:259
  7.2 2.2 %collective-permute-start.3 = (bf16[80,1152]{1,0:T(8,128)(2,1)S(1)}, bf16[80,1152]{1,0:T(8,128)(2,1)S(1)}, u32[]{:S(2)}, u32[]{:S(2)}) collective-permute-start(bf16[80,1152]{1,0:T(8,128)(2,1)S(1)} %get-tuple-element.26.target_ref), channel_id=1, source_target_pairs={{0,4},{4,0},{8,12},{12,8},{1,5},{5,1},{9,13},{13,9},{2,6},{6,2},{1... | collective-permute-start | bytes 552968 | tf_op jit(solution)/shard_map/ppermute | solution.py:259
  9.6 1.4 %collective-permute-start.1 = (bf16[64,1152]{1,0:T(8,128)(2,1)S(1)}, bf16[64,1152]{1,0:T(8,128)(2,1)S(1)}, u32[]{:S(2)}, u32[]{:S(2)}) collective-permute-start(bf16[64,1152]{1,0:T(8,128)(2,1)S(1)} %select_convert_fusion.1), channel_id=1, source_target_pairs={{0,2},{1,3},{2,0},{3,1},{4,6},{5,7},{6,4},{7,5},{8,10},{9,11},{10,... | collective-permute-start | bytes 442376 | tf_op jit(solution)/shard_map/ppermute | solution.py:259
  11.0 3.5 %collective-permute-done.3 = bf16[80,1152]{1,0:T(8,128)(2,1)S(1)} collective-permute-done((bf16[80,1152]{1,0:T(8,128)(2,1)S(1)}, bf16[80,1152]{1,0:T(8,128)(2,1)S(1)}, u32[]{:S(2)}, u32[]{:S(2)}) %collective-permute-start.3) | collective-permute-done | bytes 184352 | tf_op jit(solution)/shard_map/ppermute | solution.py:259
  14.5 0.9 %collective-permute-done.1 = bf16[64,1152]{1,0:T(8,128)(2,1)S(1)} collective-permute-done((bf16[64,1152]{1,0:T(8,128)(2,1)S(1)}, bf16[64,1152]{1,0:T(8,128)(2,1)S(1)}, u32[]{:S(2)}, u32[]{:S(2)}) %collective-permute-start.1) | collective-permute-done | bytes 147488 | tf_op jit(solution)/shard_map/ppermute | solution.py:259
  15.4 1.6 %collective-permute-start.2 = (bf16[64,1152]{1,0:T(8,128)(2,1)S(1)}, bf16[64,1152]{1,0:T(8,128)(2,1)S(1)}, u32[]{:S(2)}, u32[]{:S(2)}) collective-permute-start(bf16[64,1152]{1,0:T(8,128)(2,1)S(1)} %get-tuple-element.49), channel_id=1, source_target_pairs={{0,4},{4,0},{8,12},{12,8},{1,5},{5,1},{9,13},{13,9},{2,6},{6,2},{1... | collective-permute-start | bytes 442376 | tf_op jit(solution)/shard_map/ppermute | solution.py:259
  17.1 2.2 %collective-permute-start.5 = (f32[1,1152]{1,0:T(1,128)S(1)}, f32[1,1152]{1,0:T(1,128)S(1)}, u32[]{:S(2)}, u32[]{:S(2)}) collective-permute-start(f32[1,1152]{1,0:T(1,128)S(1)} %get-tuple-element.52), channel_id=1, source_target_pairs={{0,8},{4,12},{8,0},{12,4},{1,9},{5,13},{9,1},{13,5},{2,10},{6,14},... | collective-permute-start | bytes 13832 | tf_op jit(solution)/shard_map/ppermute | solution.py:259
  19.3 1.4 %collective-permute-done.2 = bf16[64,1152]{1,0:T(8,128)(2,1)S(1)} collective-permute-done((bf16[64,1152]{1,0:T(8,128)(2,1)S(1)}, bf16[64,1152]{1,0:T(8,128)(2,1)S(1)}, u32[]{:S(2)}, u32[]{:S(2)}) %collective-permute-start.2) | collective-permute-done | bytes 147488 | tf_op jit(solution)/shard_map/ppermute | solution.py:259
  20.7 0.2 select_convert_fusion
  20.9 2.9 %collective-permute-start.4 = (bf16[64,1152]{1,0:T(8,128)(2,1)S(1)}, bf16[64,1152]{1,0:T(8,128)(2,1)S(1)}, u32[]{:S(2)}, u32[]{:S(2)}) collective-permute-start(bf16[64,1152]{1,0:T(8,128)(2,1)S(1)} %select_convert_fusion), channel_id=1, source_target_pairs={{0,8},{4,12},{8,0},{12,4},{1,9},{5,13},{9,1},{13,5},{2,10},{6,14},... | collective-permute-start | bytes 442376 | tf_op jit(solution)/shard_map/ppermute | solution.py:259
  23.8 0.2 broadcast_select_fusion
  24.0 5.2 %collective-permute-done.4.got_ref = bf16[64,1152]{1,0:T(8,128)(2,1)S(1)} collective-permute-done((bf16[64,1152]{1,0:T(8,128)(2,1)S(1)}, bf16[64,1152]{1,0:T(8,128)(2,1)S(1)}, u32[]{:S(2)}, u32[]{:S(2)}) %collective-permute-start.4) | collective-permute-done | bytes 147488 | tf_op jit(solution)/shard_map/ppermute | solution.py:259
  29.2 0.2 finish.1
  29.4 2.1 %collective-permute-start.6 = (bf16[64,1280]{1,0:T(8,128)(2,1)S(1)}, bf16[64,1280]{1,0:T(8,128)(2,1)S(1)}, u32[]{:S(2)}, u32[]{:S(2)}) collective-permute-start(bf16[64,1280]{1,0:T(8,128)(2,1)S(1)} %get-tuple-element.30.own_ref), channel_id=1, source_target_pairs={{0,2},{1,3},{2,0},{3,1},{4,6},{5,7},{6,4},{7,5},{8,10},{9,11},{10,... | collective-permute-start | bytes 491528 | tf_op jit(solution)/shard_map/ppermute | solution.py:259
  31.5 0.1 collective-permute-start.7
  31.6 0.1 pad_maximum_fusion
  31.7 1.3 %collective-permute-done.7.near_ref = bf16[64,1152]{1,0:T(8,128)(2,1)S(1)} collective-permute-done((bf16[64,1152]{1,0:T(8,128)(2,1)S(1)}, bf16[64,1152]{1,0:T(8,128)(2,1)S(1)}, u32[]{:S(2)}, u32[]{:S(2)}) %collective-permute-start.7) | collective-permute-done | bytes 147488 | tf_op jit(solution)/shard_map/ppermute | solution.py:259
  32.9 1.7 %near_gradient.1 = (f32[4,128,512]{2,1,0:T(8,128)S(1)}, bf16[2,512,1152]{2,1,0:T(8,128)(2,1)S(1)}) custom-call(s32[1,17]{1,0:T(1,128)S(4)} %get-tuple-element.22.ids_ref, bf16[64,1280]{1,0:T(8,128)(2,1)S(1)} %get-tuple-element.30.own_ref, bf16[64,1152]{1,0:T(8,128)(2,1)S(1)} %collective-permute-done.7.near_ref, bf16[2048,2304]{1,0:T(8,128)(2,1)} %bitcast.9), custom_call_target="tpu_custom_call" | custom-call | tf_op jit(solution)/shard_map/near_gradient/pallas_call | solution.py:415
  34.6 0.4 %collective-permute-done.6.got_ref = bf16[64,1280]{1,0:T(8,128)(2,1)S(1)} collective-permute-done((bf16[64,1280]{1,0:T(8,128)(2,1)S(1)}, bf16[64,1280]{1,0:T(8,128)(2,1)S(1)}, u32[]{:S(2)}, u32[]{:S(2)}) %collective-permute-start.6) | collective-permute-done | bytes 163872 | tf_op jit(solution)/shard_map/ppermute | solution.py:259
  35.0 0.8 %collective-permute-start.8 = (bf16[64,1280]{1,0:T(8,128)(2,1)S(1)}, bf16[64,1280]{1,0:T(8,128)(2,1)S(1)}, u32[]{:S(2)}, u32[]{:S(2)}) collective-permute-start(bf16[64,1280]{1,0:T(8,128)(2,1)S(1)} %collective-permute-done.6.got_ref), channel_id=1, source_target_pairs={{0,1},{1,0},{2,3},{3,2},{4,5},{5,4},{6,7},{7,6},{8,9},{9,8},{10,11... | collective-permute-start | bytes 491528 | tf_op jit(solution)/shard_map/ppermute | solution.py:259
  35.8 0.1 collective-permute-start.9
  35.8 1.2 %collective-permute-done.9.other_ref = bf16[64,704]{1,0:T(8,128)(2,1)S(1)} collective-permute-done((bf16[64,704]{1,0:T(8,128)(2,1)S(1)}, bf16[64,704]{1,0:T(8,128)(2,1)S(1)}, u32[]{:S(2)}, u32[]{:S(2)}) %collective-permute-start.9) | collective-permute-done | bytes 90144 | tf_op jit(solution)/shard_map/ppermute | solution.py:259
  37.1 1.5 %code_gradient.1 = (bf16[128,2048]{1,0:T(8,128)(2,1)}, bf16[576,128]{1,0:T(8,128)(2,1)}, f32[1,1]{1,0:T(1,128)}) custom-call(s32[1,17]{1,0:T(1,128)S(4)} %get-tuple-element.22.ids_ref, bf16[64,1280]{1,0:T(8,128)(2,1)S(1)} %get-tuple-element.30.own_ref, bf16[64,1280]{1,0:T(8,128)(2,1)S(1)} %collective-permute-done.6.got_ref, ...), custom_call_target="tpu_custom_call" | custom-call | tf_op jit(solution)/shard_map/code_gradient/pallas_call | solution.py:433
  (12 shorter events, 0.3 us)
Async XLA Ops:
  4.6 4.9 %collective-permute-start = (bf16[64,2304]{1,0:T(8,128)(2,1)S(1)}, bf16[64,2304]{1,0:T(8,128)(2,1)S(1)}, u32[]{:S(2)}, u32[]{:S(2)}) collective-permute-start(bf16[64,2304]{1,0:T(8,128)(2,1)S(1)} %get-tuple-element.24), channel_id=1, source_target_pairs={{0,1},{1,0},{2,3},{3,2},{4,5},{5,4},{6,7},{7,6},{8,9},{9,8},{10,11... | collective-permute-start | bytes 884744 | tf_op jit(solution)/shard_map/ppermute | solution.py:259
  7.2 7.2 %collective-permute-start.3 = (bf16[80,1152]{1,0:T(8,128)(2,1)S(1)}, bf16[80,1152]{1,0:T(8,128)(2,1)S(1)}, u32[]{:S(2)}, u32[]{:S(2)}) collective-permute-start(bf16[80,1152]{1,0:T(8,128)(2,1)S(1)} %get-tuple-element.26.target_ref), channel_id=1, source_target_pairs={{0,4},{4,0},{8,12},{12,8},{1,5},{5,1},{9,13},{13,9},{2,6},{6,2},{1... | collective-permute-start | bytes 552968 | tf_op jit(solution)/shard_map/ppermute | solution.py:259
  9.6 5.8 %collective-permute-start.1 = (bf16[64,1152]{1,0:T(8,128)(2,1)S(1)}, bf16[64,1152]{1,0:T(8,128)(2,1)S(1)}, u32[]{:S(2)}, u32[]{:S(2)}) collective-permute-start(bf16[64,1152]{1,0:T(8,128)(2,1)S(1)} %select_convert_fusion.1), channel_id=1, source_target_pairs={{0,2},{1,3},{2,0},{3,1},{4,6},{5,7},{6,4},{7,5},{8,10},{9,11},{10,... | collective-permute-start | bytes 442376 | tf_op jit(solution)/shard_map/ppermute | solution.py:259
  15.4 5.3 %collective-permute-start.2 = (bf16[64,1152]{1,0:T(8,128)(2,1)S(1)}, bf16[64,1152]{1,0:T(8,128)(2,1)S(1)}, u32[]{:S(2)}, u32[]{:S(2)}) collective-permute-start(bf16[64,1152]{1,0:T(8,128)(2,1)S(1)} %get-tuple-element.49), channel_id=1, source_target_pairs={{0,4},{4,0},{8,12},{12,8},{1,5},{5,1},{9,13},{13,9},{2,6},{6,2},{1... | collective-permute-start | bytes 442376 | tf_op jit(solution)/shard_map/ppermute | solution.py:259
  17.1 6.9 %collective-permute-start.5 = (f32[1,1152]{1,0:T(1,128)S(1)}, f32[1,1152]{1,0:T(1,128)S(1)}, u32[]{:S(2)}, u32[]{:S(2)}) collective-permute-start(f32[1,1152]{1,0:T(1,128)S(1)} %get-tuple-element.52), channel_id=1, source_target_pairs={{0,8},{4,12},{8,0},{12,4},{1,9},{5,13},{9,1},{13,5},{2,10},{6,14},... | collective-permute-start | bytes 13832 | tf_op jit(solution)/shard_map/ppermute | solution.py:259
  20.9 8.3 %collective-permute-start.4 = (bf16[64,1152]{1,0:T(8,128)(2,1)S(1)}, bf16[64,1152]{1,0:T(8,128)(2,1)S(1)}, u32[]{:S(2)}, u32[]{:S(2)}) collective-permute-start(bf16[64,1152]{1,0:T(8,128)(2,1)S(1)} %select_convert_fusion), channel_id=1, source_target_pairs={{0,8},{4,12},{8,0},{12,4},{1,9},{5,13},{9,1},{13,5},{2,10},{6,14},... | collective-permute-start | bytes 442376 | tf_op jit(solution)/shard_map/ppermute | solution.py:259
  29.4 5.6 %collective-permute-start.6 = (bf16[64,1280]{1,0:T(8,128)(2,1)S(1)}, bf16[64,1280]{1,0:T(8,128)(2,1)S(1)}, u32[]{:S(2)}, u32[]{:S(2)}) collective-permute-start(bf16[64,1280]{1,0:T(8,128)(2,1)S(1)} %get-tuple-element.30.own_ref), channel_id=1, source_target_pairs={{0,2},{1,3},{2,0},{3,1},{4,6},{5,7},{6,4},{7,5},{8,10},{9,11},{10,... | collective-permute-start | bytes 491528 | tf_op jit(solution)/shard_map/ppermute | solution.py:259
  31.5 1.4 %collective-permute-start.7 = (bf16[64,1152]{1,0:T(8,128)(2,1)S(1)}, bf16[64,1152]{1,0:T(8,128)(2,1)S(1)}, u32[]{:S(2)}, u32[]{:S(2)}) collective-permute-start(bf16[64,1152]{1,0:T(8,128)(2,1)S(1)} %slice.36), channel_id=1, source_target_pairs={{0,1},{1,0},{2,3},{3,2},{4,5},{5,4},{6,7},{7,6},{8,9},{9,8},{10,11... | collective-permute-start | bytes 442376 | tf_op jit(solution)/shard_map/ppermute | solution.py:259
  35.0 2.1 %collective-permute-start.8 = (bf16[64,1280]{1,0:T(8,128)(2,1)S(1)}, bf16[64,1280]{1,0:T(8,128)(2,1)S(1)}, u32[]{:S(2)}, u32[]{:S(2)}) collective-permute-start(bf16[64,1280]{1,0:T(8,128)(2,1)S(1)} %collective-permute-done.6.got_ref), channel_id=1, source_target_pairs={{0,1},{1,0},{2,3},{3,2},{4,5},{5,4},{6,7},{7,6},{8,9},{9,8},{10,11... | collective-permute-start | bytes 491528 | tf_op jit(solution)/shard_map/ppermute | solution.py:259
  35.8 1.3 %collective-permute-start.9 = (bf16[64,704]{1,0:T(8,128)(2,1)S(1)}, bf16[64,704]{1,0:T(8,128)(2,1)S(1)}, u32[]{:S(2)}, u32[]{:S(2)}) collective-permute-start(bf16[64,704]{1,0:T(8,128)(2,1)S(1)} %pad_maximum_fusion), channel_id=1, source_target_pairs={{0,1},{1,0},{2,3},{3,2},{4,5},{5,4},{6,7},{7,6},{8,9},{9,8},{10,11... | collective-permute-start | bytes 270344 | tf_op jit(solution)/shard_map/ppermute | solution.py:259
where the time goes:
time: 39.3 us; the launch traced here: 38.5 us
  starting transfers between devices  16 us (41%)
  waiting for transfers between devices  13.8 us (35%)
  Pallas kernels  6.67 us (17%)
  between operations  1.37 us (3%)
  other arithmetic  0.65 us (2%)
    ppermute x10, starting transfers between devices, swap(): return lax.ppermute(value, axis, [(i, i ^ bit) for i in range(size)])  16 us
    ppermute x10, waiting for transfers between devices, swap(): return lax.ppermute(value, axis, [(i, i ^ bit) for i in range(size)])  13.8 us
    pallas_call x1, Pallas kernels, encode_call(): pl.pallas_call(encode_decode, out_shape=(pltpu.VMEM((rows, model_width),...  3.29 us
    pallas_call x1, Pallas kernels, local(): pl.pallas_call(functools.partial(near_gradient, top), out_shape=(pltpu.VM...  1.67 us
    pallas_call x1, Pallas kernels, local(): pl.pallas_call(functools.partial(code_gradient, top), out_shape=(jax.Shap...  1.47 us
  transfers between devices with their start and end apart: 10, of which 7 were waited for; matrix products, arithmetic and copies ran while one was open for 2% of the time, Pallas kernels for 4%

commit v1 on v0

--- a/solution.py
+++ b/solution.py
@@ -15,7 +15,7 @@
 
 
 def encode_decode(
-    list_any, count_ref, x_any, bias_any, target_any, gain_any, enc_ref, dec_ref,
+    top, list_any, count_ref, x_any, bias_any, target_any, gain_any, enc_ref, dec_ref,
     keep_ref, send_ref, ids_ref, beside_ref, own_gain_ref,
     list_ref, x_ref, bias_ref, target_ref, gain_ref, enc_held, dec_held, codes, total, in_sem, enc_sem, dec_sem,
 ):
@@ -120,8 +120,13 @@
     lax.fori_loop(2 * fours, pairs, lambda pair, c: (encode(2 * pair, 2), c)[1], 0)
     lax.fori_loop(0, pairs, decode, 0)
 
-    keep_ref[...] = total[mine, :]
-    send_ref[...] = total[pl.ds(pl.multiple_of((1 - core) * rows, rows), rows), :].astype(BF16)
+    theirs = pl.ds(pl.multiple_of((1 - core) * rows, rows), rows)
+    cut = keep_ref.shape[1] // 2
+    here = lax.div(where & top, top)
+    for place, half in ((0, 1 - here), (1, here)):
+        columns = pl.ds(pl.multiple_of(half * cut, cut), cut)
+        keep_ref[:, place * cut : (place + 1) * cut] = total[mine, columns]
+        send_ref[:, place * cut : (place + 1) * cut] = total[theirs, columns].astype(BF16)
 
 
 def finish(
@@ -267,7 +272,7 @@
     return lax.dynamic_slice_in_dim(value, start, size, axis)
 
 
-def encode_call(block_list, block_count, x, bias, targets, gain, enc, dec, width):
+def encode_call(top, block_list, block_count, x, bias, targets, gain, enc, dec, width):
     tok_rows, model_width = x.shape
     local_latents = enc.shape[1]
     blocks = local_latents // BLOCK
@@ -277,7 +282,7 @@
     smem = pl.BlockSpec(memory_space=pltpu.SMEM)
     anyw = pl.BlockSpec(memory_space=pl.ANY)
     return pl.pallas_call(
-        encode_decode,
+        functools.partial(encode_decode, top),
         out_shape=(
             pltpu.VMEM((rows, model_width), F32),
             pltpu.VMEM((rows, model_width), BF16),
@@ -330,18 +335,21 @@
     smem = pl.BlockSpec(memory_space=pltpu.SMEM)
     anyw = pl.BlockSpec(memory_space=pl.ANY)
     keep, send, ids, beside, gain = encode_call(
-        in_hbm(block_list), block_count, in_hbm(residuals[0]), in_hbm(enc_bias), in_hbm(targets[0]), in_hbm(out_gain),
+        chip_bits[0], in_hbm(block_list), block_count, in_hbm(residuals[0]), in_hbm(enc_bias), in_hbm(targets[0]), in_hbm(out_gain),
         in_hbm(enc_weight[0]), dec_hbm, width,
     )
 
-    held = keep + swap(send, "latent", 1).astype(F32)
-    for bit in chip_bits:
+    cut = model_width // 2
+    got = swap(send, "latent", 1)
+    away = (keep[:, :cut] + got[:, :cut].astype(F32)).astype(BF16)
+    near_beside = swap(beside, "layer", 1)
+    keep, got, away = lax.optimization_barrier((keep, got, away))
+    held = keep[:, cut:] + got[:, cut:].astype(F32) + swap(away, "latent", chip_bits[0]).astype(F32)
+    for bit in chip_bits[1:]:
         half = held.shape[1] // 2
         upper = (latent & bit) != 0
         away = jnp.where(upper, held[:, :half], held[:, half:]).astype(BF16)
         mine = jnp.where(upper, held[:, half:], held[:, :half])
-        if bit == chip_bits[-1]:
-            near_beside = swap(beside, "layer", 1)
         held = mine + swap(away, "latent", bit).astype(F32)
     own = held
     near = swap(own.astype(BF16), "layer", 1).astype(F32)

time: 39.3 us -> 39.8 us (1.013)
  starting transfers between devices: 16 us -> 11.7 us
  Pallas kernels: 6.67 us -> 10.3 us
  waiting for transfers between devices: 13.8 us -> 15.1 us
    ppermute x10, starting transfers between devices: 16 us -> 11.7 us  [swap(): return lax.ppermute(value, axis, [(i, i ^ bit) for i in range(size)])]
    pallas_call x1, Pallas kernels: 3.29 us -> 5.25 us  [encode_call(): pl.pallas_call(functools.partial(encode_decode, top), out_shape=(pltpu.VM...]
    ppermute x10, waiting for transfers between devices: 13.8 us -> 15.1 us  [swap(): return lax.ppermute(value, axis, [(i, i ^ bit) for i in range(size)])]
    pallas_call x1, Pallas kernels: 1.67 us -> 2.6 us  [local(): pl.pallas_call(functools.partial(near_gradient, top), out_shape=(pltpu.VM...]
    pallas_call x1, Pallas kernels: 1.47 us -> 2.25 us  [local(): pl.pallas_call(functools.partial(code_gradient, top), out_shape=(jax.Shap...]
  transfers between devices with their start and end apart: 10 -> 10, of which waited for: 7 -> 6; matrix products, arithmetic and copies ran while one was open for 2% -> 1% of each run, Pallas kernels for 4% -> 7%
where the time goes in v1:
time: 39.8 us; the launch traced here: 39.2 us
  waiting for transfers between devices  15.1 us (38%)
  starting transfers between devices  11.7 us (29%)
  Pallas kernels  10.3 us (26%)
  between operations  1.37 us (3%)
  other arithmetic  0.62 us (2%)
    ppermute x10, waiting for transfers between devices, swap(): return lax.ppermute(value, axis, [(i, i ^ bit) for i in range(size)])  15.1 us
    ppermute x10, starting transfers between devices, swap(): return lax.ppermute(value, axis, [(i, i ^ bit) for i in range(size)])  11.7 us
    pallas_call x1, Pallas kernels, encode_call(): pl.pallas_call(functools.partial(encode_decode, top), out_shape=(pltpu.VM...  5.25 us
    pallas_call x1, Pallas kernels, local(): pl.pallas_call(functools.partial(near_gradient, top), out_shape=(pltpu.VM...  2.6 us
    pallas_call x1, Pallas kernels, local(): pl.pallas_call(functools.partial(code_gradient, top), out_shape=(jax.Shap...  2.25 us
  transfers between devices with their start and end apart: 10, of which 6 were waited for; matrix products, arithmetic and copies ran while one was open for 1% of the time, Pallas kernels for 7%

profile of v1, /device:TPU:0, one launch (start us, length us, event | category | flops | bytes accessed | tf_op | source)
XLA Modules:
  0.0 39.2 jit_solution(4737081418417740046)
XLA Ops:
  1.3 5.2 %encode_decode.1 = (f32[64,2304]{1,0:T(8,128)S(1)}, bf16[64,2304]{1,0:T(8,128)(2,1)S(1)}, s32[1,17]{1,0:T(1,128)S(4)}, bf16[80,1152]{1,0:T(8,128)(2,1)S(1)}, f32[1,1152]{1,0:T(1,128)S(1)}) custom-call(s32[1,1,24]{2,1,0:T(1,128)} %list_any.1, s32[1,1]{1,0:T(1,128)S(6)} %copy.11.count_ref, bf16[128,2304]{1,0:T(8,128)(2,1)} %bitcast.12, f32[1,2048]{1,0:T(1,128)} %bias_any.1, ...), custom_call_target="tpu_custom_call" | custom-call | tf_op jit(solution)/shard_map/encode_decode/pallas_call | solution.py:284
  6.5 0.1 collective-permute-start
  6.6 1.7 %collective-permute-start.3 = (bf16[80,1152]{1,0:T(8,128)(2,1)S(1)}, bf16[80,1152]{1,0:T(8,128)(2,1)S(1)}, u32[]{:S(2)}, u32[]{:S(2)}) collective-permute-start(bf16[80,1152]{1,0:T(8,128)(2,1)S(1)} %get-tuple-element.32.target_ref), channel_id=1, source_target_pairs={{0,4},{4,0},{8,12},{12,8},{1,5},{5,1},{9,13},{13,9},{2,6},{6,2},{1... | collective-permute-start | bytes 552968 | tf_op jit(solution)/shard_map/ppermute | solution.py:264
  8.3 2.9 %collective-permute-start.1 = (bf16[64,1152]{1,0:T(8,128)(2,1)S(1)}, bf16[64,1152]{1,0:T(8,128)(2,1)S(1)}, u32[]{:S(2)}, u32[]{:S(2)}) collective-permute-start(bf16[64,1152]{1,0:T(8,128)(2,1)S(1)} %add_convert_fusion), channel_id=1, source_target_pairs={{0,2},{1,3},{2,0},{3,1},{4,6},{5,7},{6,4},{7,5},{8,10},{9,11},{10,... | collective-permute-start | bytes 442376 | tf_op jit(solution)/shard_map/ppermute | solution.py:264
  11.2 2.4 %collective-permute-done.3 = bf16[80,1152]{1,0:T(8,128)(2,1)S(1)} collective-permute-done((bf16[80,1152]{1,0:T(8,128)(2,1)S(1)}, bf16[80,1152]{1,0:T(8,128)(2,1)S(1)}, u32[]{:S(2)}, u32[]{:S(2)}) %collective-permute-start.3) | collective-permute-done | bytes 184352 | tf_op jit(solution)/shard_map/ppermute | solution.py:264
  13.7 1.7 %collective-permute-done.1 = bf16[64,1152]{1,0:T(8,128)(2,1)S(1)} collective-permute-done((bf16[64,1152]{1,0:T(8,128)(2,1)S(1)}, bf16[64,1152]{1,0:T(8,128)(2,1)S(1)}, u32[]{:S(2)}, u32[]{:S(2)}) %collective-permute-start.1) | collective-permute-done | bytes 147488 | tf_op jit(solution)/shard_map/ppermute | solution.py:264
  15.4 0.1 fusion.3
  15.4 1.5 %collective-permute-start.2 = (bf16[64,1152]{1,0:T(8,128)(2,1)S(1)}, bf16[64,1152]{1,0:T(8,128)(2,1)S(1)}, u32[]{:S(2)}, u32[]{:S(2)}) collective-permute-start(bf16[64,1152]{1,0:T(8,128)(2,1)S(1)} %get-tuple-element.55), channel_id=1, source_target_pairs={{0,4},{4,0},{8,12},{12,8},{1,5},{5,1},{9,13},{13,9},{2,6},{6,2},{1... | collective-permute-start | bytes 442376 | tf_op jit(solution)/shard_map/ppermute | solution.py:264
  17.0 1.1 %collective-permute-start.5 = (f32[1,1152]{1,0:T(1,128)S(1)}, f32[1,1152]{1,0:T(1,128)S(1)}, u32[]{:S(2)}, u32[]{:S(2)}) collective-permute-start(f32[1,1152]{1,0:T(1,128)S(1)} %get-tuple-element.58), channel_id=1, source_target_pairs={{0,8},{4,12},{8,0},{12,4},{1,9},{5,13},{9,1},{13,5},{2,10},{6,14},... | collective-permute-start | bytes 13832 | tf_op jit(solution)/shard_map/ppermute | solution.py:264
  18.2 2.8 %collective-permute-done.2 = bf16[64,1152]{1,0:T(8,128)(2,1)S(1)} collective-permute-done((bf16[64,1152]{1,0:T(8,128)(2,1)S(1)}, bf16[64,1152]{1,0:T(8,128)(2,1)S(1)}, u32[]{:S(2)}, u32[]{:S(2)}) %collective-permute-start.2) | collective-permute-done | bytes 147488 | tf_op jit(solution)/shard_map/ppermute | solution.py:264
  21.0 0.2 select_convert_fusion
  21.1 2.5 %collective-permute-start.4 = (bf16[64,1152]{1,0:T(8,128)(2,1)S(1)}, bf16[64,1152]{1,0:T(8,128)(2,1)S(1)}, u32[]{:S(2)}, u32[]{:S(2)}) collective-permute-start(bf16[64,1152]{1,0:T(8,128)(2,1)S(1)} %select_convert_fusion), channel_id=1, source_target_pairs={{0,8},{4,12},{8,0},{12,4},{1,9},{5,13},{9,1},{13,5},{2,10},{6,14},... | collective-permute-start | bytes 442376 | tf_op jit(solution)/shard_map/ppermute | solution.py:264
  23.7 0.2 broadcast_select_fusion
  23.8 5.9 %collective-permute-done.4.got_ref = bf16[64,1152]{1,0:T(8,128)(2,1)S(1)} collective-permute-done((bf16[64,1152]{1,0:T(8,128)(2,1)S(1)}, bf16[64,1152]{1,0:T(8,128)(2,1)S(1)}, u32[]{:S(2)}, u32[]{:S(2)}) %collective-permute-start.4) | collective-permute-done | bytes 147488 | tf_op jit(solution)/shard_map/ppermute | solution.py:264
  29.7 0.2 finish.1
  30.0 1.3 %collective-permute-start.6 = (bf16[64,1280]{1,0:T(8,128)(2,1)S(1)}, bf16[64,1280]{1,0:T(8,128)(2,1)S(1)}, u32[]{:S(2)}, u32[]{:S(2)}) collective-permute-start(bf16[64,1280]{1,0:T(8,128)(2,1)S(1)} %get-tuple-element.36.own_ref), channel_id=1, source_target_pairs={{0,2},{1,3},{2,0},{3,1},{4,6},{5,7},{6,4},{7,5},{8,10},{9,11},{10,... | collective-permute-start | bytes 491528 | tf_op jit(solution)/shard_map/ppermute | solution.py:264
  31.3 0.1 collective-permute-start.7
  31.3 0.1 pad_maximum_fusion
  31.4 1.3 %collective-permute-done.7.near_ref = bf16[64,1152]{1,0:T(8,128)(2,1)S(1)} collective-permute-done((bf16[64,1152]{1,0:T(8,128)(2,1)S(1)}, bf16[64,1152]{1,0:T(8,128)(2,1)S(1)}, u32[]{:S(2)}, u32[]{:S(2)}) %collective-permute-start.7) | collective-permute-done | bytes 147488 | tf_op jit(solution)/shard_map/ppermute | solution.py:264
  32.7 2.6 %near_gradient.1 = (f32[4,128,512]{2,1,0:T(8,128)S(1)}, bf16[2,512,1152]{2,1,0:T(8,128)(2,1)S(1)}) custom-call(s32[1,17]{1,0:T(1,128)S(4)} %get-tuple-element.25.ids_ref, bf16[64,1280]{1,0:T(8,128)(2,1)S(1)} %get-tuple-element.36.own_ref, bf16[64,1152]{1,0:T(8,128)(2,1)S(1)} %collective-permute-done.7.near_ref, bf16[2048,2304]{1,0:T(8,128)(2,1)} %bitcast.9), custom_call_target="tpu_custom_call" | custom-call | tf_op jit(solution)/shard_map/near_gradient/pallas_call | solution.py:423
  35.3 0.0 collective-permute-done.6.got_ref
  35.4 0.5 %collective-permute-start.9 = (bf16[64,704]{1,0:T(8,128)(2,1)S(1)}, bf16[64,704]{1,0:T(8,128)(2,1)S(1)}, u32[]{:S(2)}, u32[]{:S(2)}) collective-permute-start(bf16[64,704]{1,0:T(8,128)(2,1)S(1)} %pad_maximum_fusion), channel_id=1, source_target_pairs={{0,1},{1,0},{2,3},{3,2},{4,5},{5,4},{6,7},{7,6},{8,9},{9,8},{10,11... | collective-permute-start | bytes 270344 | tf_op jit(solution)/shard_map/ppermute | solution.py:264
  35.9 1.0 %collective-permute-done.9.other_ref = bf16[64,704]{1,0:T(8,128)(2,1)S(1)} collective-permute-done((bf16[64,704]{1,0:T(8,128)(2,1)S(1)}, bf16[64,704]{1,0:T(8,128)(2,1)S(1)}, u32[]{:S(2)}, u32[]{:S(2)}) %collective-permute-start.9) | collective-permute-done | bytes 90144 | tf_op jit(solution)/shard_map/ppermute | solution.py:264
  36.9 2.2 %code_gradient.1 = (bf16[128,2048]{1,0:T(8,128)(2,1)}, bf16[576,128]{1,0:T(8,128)(2,1)}, f32[1,1]{1,0:T(1,128)}) custom-call(s32[1,17]{1,0:T(1,128)S(4)} %get-tuple-element.25.ids_ref, bf16[64,1280]{1,0:T(8,128)(2,1)S(1)} %get-tuple-element.36.own_ref, bf16[64,1280]{1,0:T(8,128)(2,1)S(1)} %collective-permute-done.6.got_ref, ...), custom_call_target="tpu_custom_call" | custom-call | tf_op jit(solution)/shard_map/code_gradient/pallas_call | solution.py:441
  (11 shorter events, 0.2 us)
Async XLA Ops:
  6.5 1.8 %collective-permute-start = (bf16[64,2304]{1,0:T(8,128)(2,1)S(1)}, bf16[64,2304]{1,0:T(8,128)(2,1)S(1)}, u32[]{:S(2)}, u32[]{:S(2)}) collective-permute-start(bf16[64,2304]{1,0:T(8,128)(2,1)S(1)} %get-tuple-element.27), channel_id=1, source_target_pairs={{0,1},{1,0},{2,3},{3,2},{4,5},{5,4},{6,7},{7,6},{8,9},{9,8},{10,11... | collective-permute-start | bytes 884744 | tf_op jit(solution)/shard_map/ppermute | solution.py:264
  6.6 7.1 %collective-permute-start.3 = (bf16[80,1152]{1,0:T(8,128)(2,1)S(1)}, bf16[80,1152]{1,0:T(8,128)(2,1)S(1)}, u32[]{:S(2)}, u32[]{:S(2)}) collective-permute-start(bf16[80,1152]{1,0:T(8,128)(2,1)S(1)} %get-tuple-element.32.target_ref), channel_id=1, source_target_pairs={{0,4},{4,0},{8,12},{12,8},{1,5},{5,1},{9,13},{13,9},{2,6},{6,2},{1... | collective-permute-start | bytes 552968 | tf_op jit(solution)/shard_map/ppermute | solution.py:264
  8.3 7.1 %collective-permute-start.1 = (bf16[64,1152]{1,0:T(8,128)(2,1)S(1)}, bf16[64,1152]{1,0:T(8,128)(2,1)S(1)}, u32[]{:S(2)}, u32[]{:S(2)}) collective-permute-start(bf16[64,1152]{1,0:T(8,128)(2,1)S(1)} %add_convert_fusion), channel_id=1, source_target_pairs={{0,2},{1,3},{2,0},{3,1},{4,6},{5,7},{6,4},{7,5},{8,10},{9,11},{10,... | collective-permute-start | bytes 442376 | tf_op jit(solution)/shard_map/ppermute | solution.py:264
  15.4 5.5 %collective-permute-start.2 = (bf16[64,1152]{1,0:T(8,128)(2,1)S(1)}, bf16[64,1152]{1,0:T(8,128)(2,1)S(1)}, u32[]{:S(2)}, u32[]{:S(2)}) collective-permute-start(bf16[64,1152]{1,0:T(8,128)(2,1)S(1)} %get-tuple-element.55), channel_id=1, source_target_pairs={{0,4},{4,0},{8,12},{12,8},{1,5},{5,1},{9,13},{13,9},{2,6},{6,2},{1... | collective-permute-start | bytes 442376 | tf_op jit(solution)/shard_map/ppermute | solution.py:264
  17.0 6.8 %collective-permute-start.5 = (f32[1,1152]{1,0:T(1,128)S(1)}, f32[1,1152]{1,0:T(1,128)S(1)}, u32[]{:S(2)}, u32[]{:S(2)}) collective-permute-start(f32[1,1152]{1,0:T(1,128)S(1)} %get-tuple-element.58), channel_id=1, source_target_pairs={{0,8},{4,12},{8,0},{12,4},{1,9},{5,13},{9,1},{13,5},{2,10},{6,14},... | collective-permute-start | bytes 13832 | tf_op jit(solution)/shard_map/ppermute | solution.py:264
  21.1 8.6 %collective-permute-start.4 = (bf16[64,1152]{1,0:T(8,128)(2,1)S(1)}, bf16[64,1152]{1,0:T(8,128)(2,1)S(1)}, u32[]{:S(2)}, u32[]{:S(2)}) collective-permute-start(bf16[64,1152]{1,0:T(8,128)(2,1)S(1)} %select_convert_fusion), channel_id=1, source_target_pairs={{0,8},{4,12},{8,0},{12,4},{1,9},{5,13},{9,1},{13,5},{2,10},{6,14},... | collective-permute-start | bytes 442376 | tf_op jit(solution)/shard_map/ppermute | solution.py:264
  30.0 5.4 %collective-permute-start.6 = (bf16[64,1280]{1,0:T(8,128)(2,1)S(1)}, bf16[64,1280]{1,0:T(8,128)(2,1)S(1)}, u32[]{:S(2)}, u32[]{:S(2)}) collective-permute-start(bf16[64,1280]{1,0:T(8,128)(2,1)S(1)} %get-tuple-element.36.own_ref), channel_id=1, source_target_pairs={{0,2},{1,3},{2,0},{3,1},{4,6},{5,7},{6,4},{7,5},{8,10},{9,11},{10,... | collective-permute-start | bytes 491528 | tf_op jit(solution)/shard_map/ppermute | solution.py:264
  31.3 1.4 %collective-permute-start.7 = (bf16[64,1152]{1,0:T(8,128)(2,1)S(1)}, bf16[64,1152]{1,0:T(8,128)(2,1)S(1)}, u32[]{:S(2)}, u32[]{:S(2)}) collective-permute-start(bf16[64,1152]{1,0:T(8,128)(2,1)S(1)} %slice.42), channel_id=1, source_target_pairs={{0,1},{1,0},{2,3},{3,2},{4,5},{5,4},{6,7},{7,6},{8,9},{9,8},{10,11... | collective-permute-start | bytes 442376 | tf_op jit(solution)/shard_map/ppermute | solution.py:264
  35.3 1.6 %collective-permute-start.8 = (bf16[64,1280]{1,0:T(8,128)(2,1)S(1)}, bf16[64,1280]{1,0:T(8,128)(2,1)S(1)}, u32[]{:S(2)}, u32[]{:S(2)}) collective-permute-start(bf16[64,1280]{1,0:T(8,128)(2,1)S(1)} %collective-permute-done.6.got_ref), channel_id=1, source_target_pairs={{0,1},{1,0},{2,3},{3,2},{4,5},{5,4},{6,7},{7,6},{8,9},{9,8},{10,11... | collective-permute-start | bytes 491528 | tf_op jit(solution)/shard_map/ppermute | solution.py:264
  35.4 1.5 %collective-permute-start.9 = (bf16[64,704]{1,0:T(8,128)(2,1)S(1)}, bf16[64,704]{1,0:T(8,128)(2,1)S(1)}, u32[]{:S(2)}, u32[]{:S(2)}) collective-permute-start(bf16[64,704]{1,0:T(8,128)(2,1)S(1)} %pad_maximum_fusion), channel_id=1, source_target_pairs={{0,1},{1,0},{2,3},{3,2},{4,5},{5,4},{6,7},{7,6},{8,9},{9,8},{10,11... | collective-permute-start | bytes 270344 | tf_op jit(solution)/shard_map/ppermute | solution.py:264

commit v2 on v1

--- a/solution.py
+++ b/solution.py
@@ -352,7 +352,9 @@
         mine = jnp.where(upper, held[:, half:], held[:, :half])
         held = mine + swap(away, "latent", bit).astype(F32)
     own = held
-    near = swap(own.astype(BF16), "layer", 1).astype(F32)
+    sent = own.astype(BF16)
+    near = swap(sent, "layer", 1).astype(F32)
+    own, sent, near_beside = lax.optimization_barrier((own, sent, near_beside))
     target = beside[:rows]
     near_target = near_beside[:rows]
     near_gain = sum(near_beside[rows + i : rows + i + 1].astype(F32) for i in range(3))
@@ -378,6 +380,11 @@
         if step == layer_bits[-1]:
             outgoing = jnp.where((layer & step) == 0, all_before, all_after).astype(BF16)
             if len(layer_bits) == 2:
+                error_terms = square * own - gain * target.astype(F32) - near_gain * near_target.astype(F32)
+                fixed = jnp.where((layer & step) == 0, own, error_terms + jnp.where(low, near_square * own, 0.0))
+                factor = jnp.where((layer & step) == 0, 1.0, near_square + jnp.where(low, 0.0, square))
+                fixed, factor = lax.optimization_barrier((fixed, factor))
+                outgoing = (fixed + factor * near).astype(BF16)
                 own, near, outgoing = lax.optimization_barrier((own, near, outgoing))
                 before, after, all_before, _ = pair_sums(own, near)
             got = swap(outgoing, "layer", step)

time: 39.8 us -> 39.1 us (0.982)
  waiting for transfers between devices: 15.1 us -> 16.6 us
  starting transfers between devices: 11.7 us -> 10.7 us
  Pallas kernels: 10.3 us -> 9.39 us
    ppermute x10, waiting for transfers between devices: 15.1 us -> 16.6 us  [swap(): return lax.ppermute(value, axis, [(i, i ^ bit) for i in range(size)])]
    ppermute x10, starting transfers between devices: 11.7 us -> 10.7 us  [swap(): return lax.ppermute(value, axis, [(i, i ^ bit) for i in range(size)])]
    pallas_call x1, Pallas kernels: 5.25 us -> 4.74 us  [encode_call(): pl.pallas_call(functools.partial(encode_decode, top), out_shape=(pltpu.VM...]
  transfers between devices with their start and end apart: 10 -> 10, of which waited for: 6 -> 8; matrix products, arithmetic and copies ran while one was open for 1% -> 2% of each run, Pallas kernels for 7% -> 6%
where the time goes in v2:
time: 39.1 us; the launch traced here: 38.7 us
  waiting for transfers between devices  16.6 us (42%)
  starting transfers between devices  10.7 us (27%)
  Pallas kernels  9.39 us (24%)
  between operations  1.38 us (4%)
  other arithmetic  0.62 us (2%)
    ppermute x10, waiting for transfers between devices, swap(): return lax.ppermute(value, axis, [(i, i ^ bit) for i in range(size)])  16.6 us
    ppermute x10, starting transfers between devices, swap(): return lax.ppermute(value, axis, [(i, i ^ bit) for i in range(size)])  10.7 us
    pallas_call x1, Pallas kernels, encode_call(): pl.pallas_call(functools.partial(encode_decode, top), out_shape=(pltpu.VM...  4.74 us
    pallas_call x1, Pallas kernels, local(): pl.pallas_call(functools.partial(near_gradient, top), out_shape=(pltpu.VM...  2.39 us
    pallas_call x1, Pallas kernels, local(): pl.pallas_call(functools.partial(code_gradient, top), out_shape=(jax.Shap...  2.02 us
  transfers between devices with their start and end apart: 10, of which 8 were waited for; matrix products, arithmetic and copies ran while one was open for 2% of the time, Pallas kernels for 6%

profile of v2, /device:TPU:0, one launch (start us, length us, event | category | flops | bytes accessed | tf_op | source)
XLA Modules:
  0.0 38.7 jit_solution(6450825779997908909)
XLA Ops:
  1.3 4.7 %encode_decode.1 = (f32[64,2304]{1,0:T(8,128)S(1)}, bf16[64,2304]{1,0:T(8,128)(2,1)S(1)}, s32[1,17]{1,0:T(1,128)S(4)}, bf16[80,1152]{1,0:T(8,128)(2,1)S(1)}, f32[1,1152]{1,0:T(1,128)S(1)}) custom-call(s32[1,1,24]{2,1,0:T(1,128)} %list_any.1, s32[1,1]{1,0:T(1,128)S(6)} %copy.11.count_ref, bf16[128,2304]{1,0:T(8,128)(2,1)} %bitcast.12, f32[1,2048]{1,0:T(1,128)} %bias_any.1, ...), custom_call_target="tpu_custom_call" | custom-call | tf_op jit(solution)/shard_map/encode_decode/pallas_call | solution.py:284
  6.0 0.1 collective-permute-start
  6.1 1.6 %collective-permute-done = bf16[64,2304]{1,0:T(8,128)(2,1)S(1)} collective-permute-done((bf16[64,2304]{1,0:T(8,128)(2,1)S(1)}, bf16[64,2304]{1,0:T(8,128)(2,1)S(1)}, u32[]{:S(2)}, u32[]{:S(2)}) %collective-permute-start) | collective-permute-done | bytes 294944 | tf_op jit(solution)/shard_map/ppermute | solution.py:264
  7.7 3.7 %collective-permute-start.1 = (bf16[64,1152]{1,0:T(8,128)(2,1)S(1)}, bf16[64,1152]{1,0:T(8,128)(2,1)S(1)}, u32[]{:S(2)}, u32[]{:S(2)}) collective-permute-start(bf16[64,1152]{1,0:T(8,128)(2,1)S(1)} %add_convert_fusion.1), channel_id=1, source_target_pairs={{0,2},{1,3},{2,0},{3,1},{4,6},{5,7},{6,4},{7,5},{8,10},{9,11},{10,... | collective-permute-start | bytes 442376 | tf_op jit(solution)/shard_map/ppermute | solution.py:264
  11.4 0.1 collective-permute-start.2
  11.5 4.1 %collective-permute-done.1 = bf16[64,1152]{1,0:T(8,128)(2,1)S(1)} collective-permute-done((bf16[64,1152]{1,0:T(8,128)(2,1)S(1)}, bf16[64,1152]{1,0:T(8,128)(2,1)S(1)}, u32[]{:S(2)}, u32[]{:S(2)}) %collective-permute-start.1) | collective-permute-done | bytes 147488 | tf_op jit(solution)/shard_map/ppermute | solution.py:264
  15.6 1.2 %collective-permute-start.3 = (bf16[64,1152]{1,0:T(8,128)(2,1)S(1)}, bf16[64,1152]{1,0:T(8,128)(2,1)S(1)}, u32[]{:S(2)}, u32[]{:S(2)}) collective-permute-start(bf16[64,1152]{1,0:T(8,128)(2,1)S(1)} %get-tuple-element.63), channel_id=1, source_target_pairs={{0,4},{4,0},{8,12},{12,8},{1,5},{5,1},{9,13},{13,9},{2,6},{6,2},{1... | collective-permute-start | bytes 442376 | tf_op jit(solution)/shard_map/ppermute | solution.py:264
  16.8 1.0 %collective-permute-done.2 = bf16[80,1152]{1,0:T(8,128)(2,1)S(1)} collective-permute-done((bf16[80,1152]{1,0:T(8,128)(2,1)S(1)}, bf16[80,1152]{1,0:T(8,128)(2,1)S(1)}, u32[]{:S(2)}, u32[]{:S(2)}) %collective-permute-start.2) | collective-permute-done | bytes 184352 | tf_op jit(solution)/shard_map/ppermute | solution.py:264
  17.9 1.9 %collective-permute-start.5 = (f32[1,1152]{1,0:T(1,128)S(1)}, f32[1,1152]{1,0:T(1,128)S(1)}, u32[]{:S(2)}, u32[]{:S(2)}) collective-permute-start(f32[1,1152]{1,0:T(1,128)S(1)} %get-tuple-element.66), channel_id=1, source_target_pairs={{0,8},{4,12},{8,0},{12,4},{1,9},{5,13},{9,1},{13,5},{2,10},{6,14},... | collective-permute-start | bytes 13832 | tf_op jit(solution)/shard_map/ppermute | solution.py:264
  19.8 0.1 add_select_fusion.1
  19.9 1.2 %collective-permute-done.3 = bf16[64,1152]{1,0:T(8,128)(2,1)S(1)} collective-permute-done((bf16[64,1152]{1,0:T(8,128)(2,1)S(1)}, bf16[64,1152]{1,0:T(8,128)(2,1)S(1)}, u32[]{:S(2)}, u32[]{:S(2)}) %collective-permute-start.3) | collective-permute-done | bytes 147488 | tf_op jit(solution)/shard_map/ppermute | solution.py:264
  21.2 1.9 %collective-permute-start.4 = (bf16[64,1152]{1,0:T(8,128)(2,1)S(1)}, bf16[64,1152]{1,0:T(8,128)(2,1)S(1)}, u32[]{:S(2)}, u32[]{:S(2)}) collective-permute-start(bf16[64,1152]{1,0:T(8,128)(2,1)S(1)} %add_convert_fusion), channel_id=1, source_target_pairs={{0,8},{4,12},{8,0},{12,4},{1,9},{5,13},{9,1},{13,5},{2,10},{6,14},... | collective-permute-start | bytes 442376 | tf_op jit(solution)/shard_map/ppermute | solution.py:264
  23.1 0.2 broadcast_select_fusion
  23.3 6.2 %collective-permute-done.4.got_ref = bf16[64,1152]{1,0:T(8,128)(2,1)S(1)} collective-permute-done((bf16[64,1152]{1,0:T(8,128)(2,1)S(1)}, bf16[64,1152]{1,0:T(8,128)(2,1)S(1)}, u32[]{:S(2)}, u32[]{:S(2)}) %collective-permute-start.4) | collective-permute-done | bytes 147488 | tf_op jit(solution)/shard_map/ppermute | solution.py:264
  29.5 0.2 finish.1
  29.7 1.3 %collective-permute-start.6 = (bf16[64,1280]{1,0:T(8,128)(2,1)S(1)}, bf16[64,1280]{1,0:T(8,128)(2,1)S(1)}, u32[]{:S(2)}, u32[]{:S(2)}) collective-permute-start(bf16[64,1280]{1,0:T(8,128)(2,1)S(1)} %get-tuple-element.44.own_ref), channel_id=1, source_target_pairs={{0,2},{1,3},{2,0},{3,1},{4,6},{5,7},{6,4},{7,5},{8,10},{9,11},{10,... | collective-permute-start | bytes 491528 | tf_op jit(solution)/shard_map/ppermute | solution.py:264
  31.0 0.1 collective-permute-start.7
  31.1 0.1 pad_maximum_fusion
  31.2 1.3 %collective-permute-done.7.near_ref = bf16[64,1152]{1,0:T(8,128)(2,1)S(1)} collective-permute-done((bf16[64,1152]{1,0:T(8,128)(2,1)S(1)}, bf16[64,1152]{1,0:T(8,128)(2,1)S(1)}, u32[]{:S(2)}, u32[]{:S(2)}) %collective-permute-start.7) | collective-permute-done | bytes 147488 | tf_op jit(solution)/shard_map/ppermute | solution.py:264
  32.5 2.4 %near_gradient.1 = (f32[4,128,512]{2,1,0:T(8,128)S(1)}, bf16[2,512,1152]{2,1,0:T(8,128)(2,1)S(1)}) custom-call(s32[1,17]{1,0:T(1,128)S(4)} %get-tuple-element.29.ids_ref, bf16[64,1280]{1,0:T(8,128)(2,1)S(1)} %get-tuple-element.44.own_ref, bf16[64,1152]{1,0:T(8,128)(2,1)S(1)} %collective-permute-done.7.near_ref, bf16[2048,2304]{1,0:T(8,128)(2,1)} %bitcast.9), custom_call_target="tpu_custom_call" | custom-call | tf_op jit(solution)/shard_map/near_gradient/pallas_call | solution.py:430
  34.9 0.3 collective-permute-done.6.got_ref
  35.1 0.5 %collective-permute-start.9 = (bf16[64,704]{1,0:T(8,128)(2,1)S(1)}, bf16[64,704]{1,0:T(8,128)(2,1)S(1)}, u32[]{:S(2)}, u32[]{:S(2)}) collective-permute-start(bf16[64,704]{1,0:T(8,128)(2,1)S(1)} %pad_maximum_fusion), channel_id=1, source_target_pairs={{0,1},{1,0},{2,3},{3,2},{4,5},{5,4},{6,7},{7,6},{8,9},{9,8},{10,11... | collective-permute-start | bytes 270344 | tf_op jit(solution)/shard_map/ppermute | solution.py:264
  35.6 1.0 %collective-permute-done.9.other_ref = bf16[64,704]{1,0:T(8,128)(2,1)S(1)} collective-permute-done((bf16[64,704]{1,0:T(8,128)(2,1)S(1)}, bf16[64,704]{1,0:T(8,128)(2,1)S(1)}, u32[]{:S(2)}, u32[]{:S(2)}) %collective-permute-start.9) | collective-permute-done | bytes 90144 | tf_op jit(solution)/shard_map/ppermute | solution.py:264
  36.7 2.0 %code_gradient.1 = (bf16[128,2048]{1,0:T(8,128)(2,1)}, bf16[576,128]{1,0:T(8,128)(2,1)}, f32[1,1]{1,0:T(1,128)}) custom-call(s32[1,17]{1,0:T(1,128)S(4)} %get-tuple-element.29.ids_ref, bf16[64,1280]{1,0:T(8,128)(2,1)S(1)} %get-tuple-element.44.own_ref, bf16[64,1280]{1,0:T(8,128)(2,1)S(1)} %collective-permute-done.6.got_ref, ...), custom_call_target="tpu_custom_call" | custom-call | tf_op jit(solution)/shard_map/code_gradient/pallas_call | solution.py:448
  (12 shorter events, 0.3 us)
Async XLA Ops:
  6.0 1.6 %collective-permute-start = (bf16[64,2304]{1,0:T(8,128)(2,1)S(1)}, bf16[64,2304]{1,0:T(8,128)(2,1)S(1)}, u32[]{:S(2)}, u32[]{:S(2)}) collective-permute-start(bf16[64,2304]{1,0:T(8,128)(2,1)S(1)} %get-tuple-element.31), channel_id=1, source_target_pairs={{0,1},{1,0},{2,3},{3,2},{4,5},{5,4},{6,7},{7,6},{8,9},{9,8},{10,11... | collective-permute-start | bytes 884744 | tf_op jit(solution)/shard_map/ppermute | solution.py:264
  7.7 7.9 %collective-permute-start.1 = (bf16[64,1152]{1,0:T(8,128)(2,1)S(1)}, bf16[64,1152]{1,0:T(8,128)(2,1)S(1)}, u32[]{:S(2)}, u32[]{:S(2)}) collective-permute-start(bf16[64,1152]{1,0:T(8,128)(2,1)S(1)} %add_convert_fusion.1), channel_id=1, source_target_pairs={{0,2},{1,3},{2,0},{3,1},{4,6},{5,7},{6,4},{7,5},{8,10},{9,11},{10,... | collective-permute-start | bytes 442376 | tf_op jit(solution)/shard_map/ppermute | solution.py:264
  11.4 6.4 %collective-permute-start.2 = (bf16[80,1152]{1,0:T(8,128)(2,1)S(1)}, bf16[80,1152]{1,0:T(8,128)(2,1)S(1)}, u32[]{:S(2)}, u32[]{:S(2)}) collective-permute-start(bf16[80,1152]{1,0:T(8,128)(2,1)S(1)} %get-tuple-element.35.target_ref), channel_id=1, source_target_pairs={{0,4},{4,0},{8,12},{12,8},{1,5},{5,1},{9,13},{13,9},{2,6},{6,2},{1... | collective-permute-start | bytes 552968 | tf_op jit(solution)/shard_map/ppermute | solution.py:264
  15.6 5.5 %collective-permute-start.3 = (bf16[64,1152]{1,0:T(8,128)(2,1)S(1)}, bf16[64,1152]{1,0:T(8,128)(2,1)S(1)}, u32[]{:S(2)}, u32[]{:S(2)}) collective-permute-start(bf16[64,1152]{1,0:T(8,128)(2,1)S(1)} %get-tuple-element.63), channel_id=1, source_target_pairs={{0,4},{4,0},{8,12},{12,8},{1,5},{5,1},{9,13},{13,9},{2,6},{6,2},{1... | collective-permute-start | bytes 442376 | tf_op jit(solution)/shard_map/ppermute | solution.py:264
  17.9 5.4 %collective-permute-start.5 = (f32[1,1152]{1,0:T(1,128)S(1)}, f32[1,1152]{1,0:T(1,128)S(1)}, u32[]{:S(2)}, u32[]{:S(2)}) collective-permute-start(f32[1,1152]{1,0:T(1,128)S(1)} %get-tuple-element.66), channel_id=1, source_target_pairs={{0,8},{4,12},{8,0},{12,4},{1,9},{5,13},{9,1},{13,5},{2,10},{6,14},... | collective-permute-start | bytes 13832 | tf_op jit(solution)/shard_map/ppermute | solution.py:264
  21.2 8.3 %collective-permute-start.4 = (bf16[64,1152]{1,0:T(8,128)(2,1)S(1)}, bf16[64,1152]{1,0:T(8,128)(2,1)S(1)}, u32[]{:S(2)}, u32[]{:S(2)}) collective-permute-start(bf16[64,1152]{1,0:T(8,128)(2,1)S(1)} %add_convert_fusion), channel_id=1, source_target_pairs={{0,8},{4,12},{8,0},{12,4},{1,9},{5,13},{9,1},{13,5},{2,10},{6,14},... | collective-permute-start | bytes 442376 | tf_op jit(solution)/shard_map/ppermute | solution.py:264
  29.7 5.4 %collective-permute-start.6 = (bf16[64,1280]{1,0:T(8,128)(2,1)S(1)}, bf16[64,1280]{1,0:T(8,128)(2,1)S(1)}, u32[]{:S(2)}, u32[]{:S(2)}) collective-permute-start(bf16[64,1280]{1,0:T(8,128)(2,1)S(1)} %get-tuple-element.44.own_ref), channel_id=1, source_target_pairs={{0,2},{1,3},{2,0},{3,1},{4,6},{5,7},{6,4},{7,5},{8,10},{9,11},{10,... | collective-permute-start | bytes 491528 | tf_op jit(solution)/shard_map/ppermute | solution.py:264
  31.0 1.4 %collective-permute-start.7 = (bf16[64,1152]{1,0:T(8,128)(2,1)S(1)}, bf16[64,1152]{1,0:T(8,128)(2,1)S(1)}, u32[]{:S(2)}, u32[]{:S(2)}) collective-permute-start(bf16[64,1152]{1,0:T(8,128)(2,1)S(1)} %slice.42), channel_id=1, source_target_pairs={{0,1},{1,0},{2,3},{3,2},{4,5},{5,4},{6,7},{7,6},{8,9},{9,8},{10,11... | collective-permute-start | bytes 442376 | tf_op jit(solution)/shard_map/ppermute | solution.py:264
  35.1 1.5 %collective-permute-start.8 = (bf16[64,1280]{1,0:T(8,128)(2,1)S(1)}, bf16[64,1280]{1,0:T(8,128)(2,1)S(1)}, u32[]{:S(2)}, u32[]{:S(2)}) collective-permute-start(bf16[64,1280]{1,0:T(8,128)(2,1)S(1)} %collective-permute-done.6.got_ref), channel_id=1, source_target_pairs={{0,1},{1,0},{2,3},{3,2},{4,5},{5,4},{6,7},{7,6},{8,9},{9,8},{10,11... | collective-permute-start | bytes 491528 | tf_op jit(solution)/shard_map/ppermute | solution.py:264
  35.1 1.5 %collective-permute-start.9 = (bf16[64,704]{1,0:T(8,128)(2,1)S(1)}, bf16[64,704]{1,0:T(8,128)(2,1)S(1)}, u32[]{:S(2)}, u32[]{:S(2)}) collective-permute-start(bf16[64,704]{1,0:T(8,128)(2,1)S(1)} %pad_maximum_fusion), channel_id=1, source_target_pairs={{0,1},{1,0},{2,3},{3,2},{4,5},{5,4},{6,7},{7,6},{8,9},{9,8},{10,11... | collective-permute-start | bytes 270344 | tf_op jit(solution)/shard_map/ppermute | solution.py:264
